TPU v7x, 32 devices: a whole 2x2x4 slice. The times are simulated.
32 devices in a mesh: diag: 16 (over z, y, x), off: 2 (over core).
Axes of the slice: x: 2, y: 2, z: 4, core: 2. Of those that a mesh axis runs over, the one named last changes fastest.
Arguments:
- trunk: bfloat16 [16, 1, 64, 128], P('diag'), may hold values from -6 to 6
- w_first: bfloat16 [48, 128, 3, 3], replicated, may hold values from -0.1875 to 0.1875
- b_first: float32 [48], replicated, may hold values from -3 to 3
- w_second: bfloat16 [48, 48, 3, 3], replicated, may hold values from -0.3125 to 0.3125
- b_second: float32 [48], replicated, may hold values from -3 to 3
Outputs:
- contact_tiles: bfloat16 [16, 2, 1, 48, 128, 128], P('diag', 'off')
All inputs are finite; a program needn't handle non-finite values.
Results may differ from a plain program's by a relative error of at most 0.0043.
Values may be sent and summed in bfloat16 or wider, within the bound.
A program may use at most 128 MiB of HBM per device.

v0:
```python
import jax
import jax.numpy as jnp
from jax import lax
from jax.sharding import PartitionSpec as P


def from_behind(shard, axis, by):
    length = lax.axis_size(axis)
    pairs = [(i, i + by) for i in range(length) if 0 <= i + by < length]
    return lax.ppermute(shard, axis, pairs)


def band_mask(row_tile, col_tile, start, extent, width, nbins, offsets_total):
    offsets = start + jnp.arange(extent, dtype=jnp.int32)
    row_bins = row_tile * width + offsets
    col_bins = col_tile * width + offsets
    row_ok = (row_bins >= 0) & (row_bins < nbins)
    col_ok = (col_bins >= 0) & (col_bins < nbins)
    gap = jnp.floor_divide(col_bins, width)[None, :] - jnp.floor_divide(row_bins, width)[:, None]
    return row_ok[:, None] & col_ok[None, :] & (gap >= 0) & (gap < offsets_total)


def neighbour(piece, by, keep):
    moved = from_behind(piece, ("diag", "off"), by)
    return jnp.where(keep, moved, jnp.zeros_like(moved))


def local(trunk, w_first, b_first, w_second, b_second):
    samples = trunk.shape[1]
    channels = trunk.shape[2]
    width = trunk.shape[3]
    hidden_width = w_first.shape[0]
    offsets_total = lax.axis_size("off")
    nbins = lax.axis_size("diag") * width
    row_tile = lax.axis_index("diag")
    offset = lax.axis_index("off")
    col_tile = row_tile + offset
    ahead = trunk
    length = 1
    while length < offsets_total + 1:
        moved = from_behind(ahead, "diag", -length)
        ahead = jnp.concatenate([ahead, moved], axis=0)
        length = length * 2
    below = from_behind(trunk, "diag", 1)
    window = jnp.concatenate([below, ahead[: offsets_total + 1]], axis=0)
    line = jnp.transpose(window, (1, 2, 0, 3)).reshape(
        samples, channels, (offsets_total + 2) * width
    )
    reach = 2
    extent = width + 2 * reach
    inner_size = extent - 4
    rows = line[:, :, width - reach : width - reach + extent]
    cols = lax.dynamic_slice_in_dim(line, (1 + offset) * width - reach, extent, 2)
    outer_mask = band_mask(row_tile, col_tile, -reach, extent, width, nbins, offsets_total)
    pre = jnp.zeros((samples, hidden_width, inner_size, inner_size), jnp.float32)
    features = jnp.concatenate(
        [
            jnp.broadcast_to(rows[:, :, :, None], (samples, channels, extent, extent)),
            jnp.broadcast_to(cols[:, :, None, :], (samples, channels, extent, extent)),
        ],
        axis=1,
    )
    features = jnp.where(outer_mask[None, None], features, jnp.zeros_like(features))
    for tap_row in range(3):
        for tap_col in range(3):
            window_cells = features[
                :, :, 2 * tap_row : 2 * tap_row + inner_size, 2 * tap_col : 2 * tap_col + inner_size
            ]
            pre = pre + jnp.einsum(
                "hc,bcij->bhij",
                w_first[:, :, tap_row, tap_col],
                window_cells,
                preferred_element_type=jnp.float32,
            )
    inner_mask = band_mask(row_tile, col_tile, 2 - reach, inner_size, width, nbins, offsets_total)
    hidden = jnp.where(
        inner_mask[None, None], jnp.maximum(pre + b_first[None, :, None, None], 0.0), 0.0
    )
    hidden = hidden.astype(jnp.bfloat16)
    low_rows = hidden[:, :, width - 4 :, :]
    high_rows = hidden[:, :, :4, :]
    top_left = neighbour(low_rows[:, :, :, width - 4 :], offsets_total, True)
    top_mid = neighbour(low_rows, offsets_total - 1, offset < offsets_total - 1)
    bottom_mid = neighbour(high_rows, -(offsets_total - 1), offset > 0)
    bottom_right = neighbour(high_rows[:, :, :, :4], -offsets_total, True)
    if offsets_total > 2:
        top_right = neighbour(low_rows[:, :, :, :4], offsets_total - 2, offset < offsets_total - 2)
        bottom_left = neighbour(high_rows[:, :, :, width - 4 :], -(offsets_total - 2), offset > 1)
    else:
        top_right = jnp.zeros_like(top_left)
        bottom_left = jnp.zeros_like(top_left)
    left = neighbour(hidden[:, :, :, width - 4 :], 1, offset > 0)
    right = neighbour(hidden[:, :, :, :4], -1, offset < offsets_total - 1)
    upper = jnp.concatenate([top_left, top_mid, top_right], axis=3)
    middle = jnp.concatenate([left, hidden, right], axis=3)
    lower = jnp.concatenate([bottom_left, bottom_mid, bottom_right], axis=3)
    hidden = jnp.concatenate([upper, middle, lower], axis=2)
    result = jnp.zeros((samples, hidden_width, width, width), jnp.float32)
    for tap_row in range(3):
        for tap_col in range(3):
            window_cells = hidden[
                :, :, 4 * tap_row : 4 * tap_row + width, 4 * tap_col : 4 * tap_col + width
            ]
            result = result + jnp.einsum(
                "hk,bkij->bhij",
                w_second[:, :, tap_row, tap_col],
                window_cells,
                preferred_element_type=jnp.float32,
            )
    result = (result + b_second[None, :, None, None]).astype(jnp.bfloat16)
    return result[None, None]


def solution(mesh):
    placed = (P("diag", None, None, None), P(), P(), P(), P())
    return jax.shard_map(
        local,
        mesh=mesh,
        in_specs=placed,
        out_specs=P("diag", "off", None, None, None, None),
        check_vma=False,
    )
```

profile of v0, /device:TPU:24, one launch (start us, length us, event | category | flops | bytes accessed | tf_op | source)
XLA Modules:
  0.0 114.3 jit_solution(17994273595948523670)
XLA Ops:
  0.0 4.2 %collective-permute-start.1 = (bf16[1,1,64,128]{3,2,1,0:T(8,128)(2,1)}, bf16[1,1,64,128]{3,2,1,0:T(8,128)(2,1)S(1)}, u32[]{:S(2)}, u32[]{:S(2)}) collective-permute-start(bf16[1,1,64,128]{3,2,1,0:T(8,128)(2,1)} %param.5), channel_id=1, source_target_pairs={{2,0},{4,2},{6,4},{8,6},{10,8},{12,10},{14,12},{16,14},{18,16},{20... | collective-permute-start | bytes 49160 | tf_op jit(solution)/shard_map/ppermute | solution.py:10
  4.2 1.9 %collective-permute-start = (bf16[1,1,64,128]{3,2,1,0:T(8,128)(2,1)}, bf16[1,1,64,128]{3,2,1,0:T(8,128)(2,1)S(1)}, u32[]{:S(2)}, u32[]{:S(2)}) collective-permute-start(bf16[1,1,64,128]{3,2,1,0:T(8,128)(2,1)} %param.5), channel_id=1, source_target_pairs={{0,2},{2,4},{4,6},{6,8},{8,10},{10,12},{12,14},{14,16},{16,18},{18... | collective-permute-start | bytes 49160 | tf_op jit(solution)/shard_map/ppermute | solution.py:10
  6.2 0.1 fusion.30
  6.4 0.7 pad_maximum_fusion.4
  7.1 3.0 %collective-permute-start.2 = (bf16[2,1,64,128]{3,2,1,0:T(8,128)(2,1)S(1)}, bf16[2,1,64,128]{3,2,1,0:T(8,128)(2,1)S(1)}, u32[]{:S(2)}, u32[]{:S(2)}) collective-permute-start(bf16[2,1,64,128]{3,2,1,0:T(8,128)(2,1)S(1)} %pad_maximum_fusion.4), channel_id=1, source_target_pairs={{4,0},{6,2},{8,4},{10,6},{12,8},{14,10},{16,12},{18,14},{20,16},{2... | collective-permute-start | bytes 98312 | tf_op jit(solution)/shard_map/ppermute | solution.py:10
  10.2 1.7 %collective-permute-done = bf16[1,1,64,128]{3,2,1,0:T(8,128)(2,1)S(1)} collective-permute-done((bf16[1,1,64,128]{3,2,1,0:T(8,128)(2,1)}, bf16[1,1,64,128]{3,2,1,0:T(8,128)(2,1)S(1)}, u32[]{:S(2)}, u32[]{:S(2)}) %collective-permute-start) | collective-permute-done | bytes 16416 | tf_op jit(solution)/shard_map/ppermute | solution.py:10
  11.9 1.0 collective-permute-done.2
  12.9 0.7 copy_bitcast_fusion
  13.7 0.1 copy.12
  13.8 1.6 %broadcast_in_dim.29 = bf16[1,64,132,132]{3,1,2,0:T(8,128)(2,1)S(1)} broadcast(bf16[64,132]{0,1:T(8,128)(2,1)S(1)} %copy.12), dimensions={1,2} | broadcast | bytes 2247168 | tf_op jit(solution)/shard_map/broadcast_in_dim | solution.py:58
  15.4 0.5 broadcast_in_dim.35
  16.0 2.8 %maximum_select_fusion = bf16[1,128,132,132]{3,1,2,0:T(8,128)(2,1)S(1)} fusion(bf16[1,64,132,132]{3,1,2,0:T(8,128)(2,1)S(1)} %broadcast_in_dim.35, bf16[1,64,132,132]{3,1,2,0:T(8,128)(2,1)S(1)} %broadcast_in_dim.29, pred[132,132]{1,0:T(8,128)(4,1)S(1)} %fusion.30), kind=kLoop, calls=%fused_computation | loop fusion | flops 11151360 | bytes 8938512 | tf_op jit(solution)/shard_map/jit(_where)/select_n | solution.py:63
  18.8 1.6 %fusion = f32[128,128,48]{1,2,0:T(8,128)S(1)} fusion(bf16[1,128,132,132]{3,1,2,0:T(8,128)(2,1)S(1)} %maximum_select_fusion, bf16[48,128,3,3]{1,0,3,2:T(8,128)(2,1)S(1)} %copy-done.3), kind=kOutput, calls=%fused_computation.2 | convolution fusion | flops 201326592 | bytes 7352320 | tf_op jit(solution)/shard_map/hc,bcij->bhij/dot_general | solution.py:69
  20.3 3.2 %fusion.1 = f32[128,128,48]{1,2,0:T(8,128)} fusion(bf16[1,128,132,132]{3,1,2,0:T(8,128)(2,1)S(1)} %maximum_select_fusion, bf16[48,128,3,3]{1,0,3,2:T(8,128)(2,1)S(1)} %copy-done.3), kind=kOutput, calls=%fused_computation.4 | convolution fusion | flops 201326592 | bytes 7352320 | tf_op jit(solution)/shard_map/hc,bcij->bhij/dot_general | solution.py:69
  23.5 2.4 %fusion.2 = f32[128,128,48]{1,2,0:T(8,128)} fusion(bf16[1,128,132,132]{3,1,2,0:T(8,128)(2,1)S(1)} %maximum_select_fusion, bf16[48,128,3,3]{1,0,3,2:T(8,128)(2,1)S(1)} %copy-done.3), kind=kOutput, calls=%fused_computation.6 | convolution fusion | flops 201326592 | bytes 7352320 | tf_op jit(solution)/shard_map/hc,bcij->bhij/dot_general | solution.py:69
  25.9 3.3 %fusion.3 = f32[128,128,48]{1,2,0:T(8,128)} fusion(bf16[1,128,132,132]{3,1,2,0:T(8,128)(2,1)S(1)} %maximum_select_fusion, bf16[48,128,3,3]{1,0,3,2:T(8,128)(2,1)S(1)} %copy-done.3), kind=kOutput, calls=%fused_computation.8 | convolution fusion | flops 201326592 | bytes 7352320 | tf_op jit(solution)/shard_map/hc,bcij->bhij/dot_general | solution.py:69
  29.2 3.2 %fusion.4 = f32[128,128,48]{1,2,0:T(8,128)} fusion(bf16[1,128,132,132]{3,1,2,0:T(8,128)(2,1)S(1)} %maximum_select_fusion, bf16[48,128,3,3]{1,0,3,2:T(8,128)(2,1)S(1)} %copy-done.3), kind=kOutput, calls=%fused_computation.10 | convolution fusion | flops 201326592 | bytes 7352320 | tf_op jit(solution)/shard_map/hc,bcij->bhij/dot_general | solution.py:69
  32.4 2.3 %fusion.5 = f32[128,128,48]{1,2,0:T(8,128)} fusion(bf16[1,128,132,132]{3,1,2,0:T(8,128)(2,1)S(1)} %maximum_select_fusion, bf16[48,128,3,3]{1,0,3,2:T(8,128)(2,1)S(1)} %copy-done.3), kind=kOutput, calls=%fused_computation.12 | convolution fusion | flops 201326592 | bytes 7352320 | tf_op jit(solution)/shard_map/hc,bcij->bhij/dot_general | solution.py:69
  34.7 3.2 %fusion.6 = f32[128,128,48]{1,2,0:T(8,128)} fusion(bf16[1,128,132,132]{3,1,2,0:T(8,128)(2,1)S(1)} %maximum_select_fusion, bf16[48,128,3,3]{1,0,3,2:T(8,128)(2,1)S(1)} %copy-done.3), kind=kOutput, calls=%fused_computation.14 | convolution fusion | flops 201326592 | bytes 7352320 | tf_op jit(solution)/shard_map/hc,bcij->bhij/dot_general | solution.py:69
  37.9 3.3 %fusion.7 = f32[128,128,48]{1,2,0:T(8,128)} fusion(bf16[1,128,132,132]{3,1,2,0:T(8,128)(2,1)S(1)} %maximum_select_fusion, bf16[48,128,3,3]{1,0,3,2:T(8,128)(2,1)S(1)} %copy-done.3), kind=kOutput, calls=%fused_computation.16 | convolution fusion | flops 201326592 | bytes 7352320 | tf_op jit(solution)/shard_map/hc,bcij->bhij/dot_general | solution.py:69
  41.2 8.7 %fusion.12 = bf16[1,128,128,48]{2,3,1,0:T(8,128)(2,1)S(1)} fusion(f32[128,128,48]{1,2,0:T(8,128)S(1)} %fusion, f32[128,128,48]{1,2,0:T(8,128)} %fusion.1, f32[128,128,48]{1,2,0:T(8,128)} %fusion.2, f32[128,128,48]{1,2,0:T(8,128)} %fusion.3, f32[128,128,48]{1,2,0:T(8,128)} %fusion.4, f32[128,128,48]{1,2,0:T(8,128)} %fusion.5, f32[128,128,48]{1,2,0:T(8,128)} %fusion.6, ...), kind=kOutput, calls=%fused_computation.26 | convolution fusion | flops 210763776 | bytes 30962176 | tf_op jit(solution)/shard_map/hc,bcij->bhij/dot_general | solution.py:69
  49.9 1.7 %fusion.77 = (bf16[1,48,128,4]{3,1,2,0:T(8,128)(2,1)}, bf16[1,48,128,4]{3,1,2,0:T(8,128)(2,1)S(1)}) fusion(bf16[1,48,128,128]{3,1,2,0:T(8,128)(2,1)S(1)} %bitcast.178), kind=kLoop, calls=%fused_computation.134 | loop fusion | bytes 196608 | tf_op jit(solution)/shard_map/slice | solution.py:92
  51.6 0.6 fusion.76
  52.2 0.7 fusion.75
  52.9 2.2 %copy.13 = bf16[1,48,128,4]{2,1,3,0:T(8,128)(2,1)S(1)} copy(bf16[1,48,128,4]{3,1,2,0:T(8,128)(2,1)} %get-tuple-element.11) | data formatting | bytes 98304 | tf_op jit(solution)/shard_map/slice | solution.py:92
  55.1 1.9 %collective-permute-start.5 = (bf16[1,48,128,4]{2,1,3,0:T(8,128)(2,1)S(1)}, bf16[1,48,128,4]{2,1,3,0:T(8,128)(2,1)S(1)}, u32[]{:S(2)}, u32[]{:S(2)}) collective-permute-start(bf16[1,48,128,4]{2,1,3,0:T(8,128)(2,1)S(1)} %copy.13), channel_id=1, source_target_pairs={{0,1},{1,2},{2,3},{3,4},{4,5},{5,6},{6,7},{7,8},{8,9},{9,10},{10,1... | collective-permute-start | bytes 147464 | tf_op jit(solution)/shard_map/ppermute | solution.py:10
  57.1 1.0 copy.15
  58.1 5.4 %collective-permute-start.6 = (bf16[1,48,128,4]{2,1,3,0:T(8,128)(2,1)S(1)}, bf16[1,48,128,4]{2,1,3,0:T(8,128)(2,1)S(1)}, u32[]{:S(2)}, u32[]{:S(2)}) collective-permute-start(bf16[1,48,128,4]{2,1,3,0:T(8,128)(2,1)S(1)} %copy.15), channel_id=1, source_target_pairs={{1,0},{2,1},{3,2},{4,3},{5,4},{6,5},{7,6},{8,7},{9,8},{10,9},{11,1... | collective-permute-start | bytes 147464 | tf_op jit(solution)/shard_map/ppermute | solution.py:10
  63.5 3.2 %collective-permute-start.7 = (bf16[1,48,4,128]{3,1,2,0:T(8,128)(2,1)}, bf16[1,48,4,128]{3,1,2,0:T(8,128)(2,1)}, u32[]{:S(2)}, u32[]{:S(2)}) collective-permute-start(bf16[1,48,4,128]{3,1,2,0:T(8,128)(2,1)} %get-tuple-element.10), channel_id=1, source_target_pairs={{1,0},{2,1},{3,2},{4,3},{5,4},{6,5},{7,6},{8,7},{9,8},{10,9},{11,1... | collective-permute-start | bytes 147464 | tf_op jit(solution)/shard_map/ppermute | solution.py:10
  66.7 1.9 %collective-permute-start.4 = (bf16[1,48,4,128]{3,1,2,0:T(8,128)(2,1)}, bf16[1,48,4,128]{3,1,2,0:T(8,128)(2,1)}, u32[]{:S(2)}, u32[]{:S(2)}) collective-permute-start(bf16[1,48,4,128]{3,1,2,0:T(8,128)(2,1)} %get-tuple-element.9), channel_id=1, source_target_pairs={{0,1},{1,2},{2,3},{3,4},{4,5},{5,6},{6,7},{7,8},{8,9},{9,10},{10,1... | collective-permute-start | bytes 147464 | tf_op jit(solution)/shard_map/ppermute | solution.py:10
  68.7 1.9 %collective-permute-start.3 = (bf16[1,48,4,4]{3,1,2,0:T(8,128)(2,1)}, bf16[1,48,4,4]{3,1,2,0:T(8,128)(2,1)S(1)}, u32[]{:S(2)}, u32[]{:S(2)}) collective-permute-start(bf16[1,48,4,4]{3,1,2,0:T(8,128)(2,1)} %get-tuple-element.7), channel_id=1, source_target_pairs={{0,2},{1,3},{2,4},{3,5},{4,6},{5,7},{6,8},{7,9},{8,10},{9,11},{10,... | collective-permute-start | bytes 4616 | tf_op jit(solution)/shard_map/ppermute | solution.py:10
  70.6 2.2 %fusion.26 = f32[128,128,48]{1,2,0:T(8,128)} fusion(bf16[1,128,128,48]{2,3,1,0:T(8,128)(2,1)S(1)} %fusion.12, bf16[48,48,3,3]{1,0,3,2:T(8,128)(2,1)S(1)} %copy-done.2), kind=kOutput, calls=%fused_computation.46 | convolution fusion | flops 75497472 | bytes 4730880 | tf_op jit(solution)/shard_map/hk,bkij->bhij/dot_general | solution.py:104
  72.8 5.7 %collective-permute-start.8 = (bf16[1,48,4,4]{3,1,2,0:T(8,128)(2,1)}, bf16[1,48,4,4]{3,1,2,0:T(8,128)(2,1)S(1)}, u32[]{:S(2)}, u32[]{:S(2)}) collective-permute-start(bf16[1,48,4,4]{3,1,2,0:T(8,128)(2,1)} %get-tuple-element.8), channel_id=1, source_target_pairs={{2,0},{3,1},{4,2},{5,3},{6,4},{7,5},{8,6},{9,7},{10,8},{11,9},{12,... | collective-permute-start | bytes 4616 | tf_op jit(solution)/shard_map/ppermute | solution.py:10
  78.5 1.7 %copy.14 = bf16[1,48,128,4]{3,1,2,0:T(8,128)(2,1)} copy(bf16[1,48,128,4]{2,1,3,0:T(8,128)(2,1)S(1)} %collective-permute-done.5) | data formatting | bytes 98304 | tf_op jit(solution)/shard_map/ppermute | solution.py:10
  80.4 2.6 %fusion.20 = f32[128,128,48]{1,2,0:T(8,128)} fusion(bf16[1,48,128,128]{3,1,2,0:T(8,128)(2,1)S(1)} %bitcast.181, bf16[1,48,128,4]{3,1,2,0:T(8,128)(2,1)S(1)} %broadcast_select_fusion.1, bf16[48,48,3,3]{1,0,3,2:T(8,128)(2,1)S(1)} %copy-done.2), kind=kOutput, calls=%fused_computation.38 | convolution fusion | flops 78643200 | bytes 6303744 | tf_op jit(solution)/shard_map/hk,bkij->bhij/dot_general | solution.py:104
  82.9 1.7 %copy.16 = bf16[1,48,128,4]{3,1,2,0:T(8,128)(2,1)} copy(bf16[1,48,128,4]{2,1,3,0:T(8,128)(2,1)S(1)} %collective-permute-done.6) | data formatting | bytes 98304 | tf_op jit(solution)/shard_map/ppermute | solution.py:10
  84.7 1.5 %broadcast_select_fusion = bf16[1,48,128,4]{3,1,2,0:T(8,128)(2,1)S(1)} fusion(bf16[1,48,128,4]{3,1,2,0:T(8,128)(2,1)} %copy.16, pred[]{:T(512)S(6)} %lt.64), kind=kLoop, calls=%fused_computation.48 | loop fusion | flops 24576 | bytes 98305 | tf_op jit(solution)/shard_map/jit(_where)/select_n | solution.py:25
  86.2 1.2 %fusion.16 = f32[128,128,48]{1,2,0:T(8,128)S(1)} fusion(bf16[1,48,128,4]{3,1,2,0:T(8,128)(2,1)S(1)} %broadcast_select_fusion, bf16[1,48,128,128]{3,1,2,0:T(8,128)(2,1)S(1)} %bitcast.182, bf16[48,48,3,3]{1,0,3,2:T(8,128)(2,1)S(1)} %copy-done.2), kind=kOutput, calls=%fused_computation.34 | convolution fusion | flops 78643200 | bytes 6303744 | tf_op jit(solution)/shard_map/hk,bkij->bhij/dot_general | solution.py:104
  87.4 0.8 broadcast_select_fusion.3
  88.2 9.7 %maximum_maximum_fusion = (bf16[1,48,132,136]{3,1,2,0:T(8,128)(2,1)S(1)}, bf16[1,48,132,136]{3,1,2,0:T(8,128)(2,1)S(1)}) fusion(bf16[1,48,128,4]{3,1,2,0:T(8,128)(2,1)S(1)} %broadcast_select_fusion, bf16[1,48,128,128]{3,1,2,0:T(8,128)(2,1)S(1)} %bitcast.183, bf16[1,48,128,4]{3,1,2,0:T(8,128)(2,1)S(1)} %broadcast_select_fusion.1, ...), kind=kLoop, calls=%fused_computation.19 | loop fusion | flops 20680704 | bytes 5220864 | tf_op jit(solution)/shard_map/concatenate | solution.py:97
  98.0 0.7 fusion.13
  98.7 0.5 fusion.14
  99.3 2.4 %fusion.23 = f32[128,128,48]{1,2,0:T(8,128)} fusion(bf16[1,48,132,136]{3,1,2,0:T(8,128)(2,1)S(1)} %get-tuple-element.5, bf16[48,48,3,3]{1,0,3,2:T(8,128)(2,1)S(1)} %copy-done.2), kind=kOutput, calls=%fused_computation.41 | convolution fusion | flops 75497472 | bytes 4730880 | tf_op jit(solution)/shard_map/hk,bkij->bhij/dot_general | solution.py:104
  101.7 2.3 %fusion.24 = f32[128,128,48]{1,2,0:T(8,128)} fusion(bf16[1,48,132,136]{3,1,2,0:T(8,128)(2,1)S(1)} %get-tuple-element.5, bf16[48,48,3,3]{1,0,3,2:T(8,128)(2,1)S(1)} %copy-done.2), kind=kOutput, calls=%fused_computation.43 | convolution fusion | flops 75497472 | bytes 4730880 | tf_op jit(solution)/shard_map/hk,bkij->bhij/dot_general | solution.py:104
  104.0 2.2 %fusion.25 = f32[128,128,48]{1,2,0:T(8,128)} fusion(bf16[1,48,132,136]{3,1,2,0:T(8,128)(2,1)S(1)} %get-tuple-element.5, bf16[48,48,3,3]{1,0,3,2:T(8,128)(2,1)S(1)} %copy-done.2), kind=kOutput, calls=%fused_computation.45 | convolution fusion | flops 75497472 | bytes 4730880 | tf_op jit(solution)/shard_map/hk,bkij->bhij/dot_general | solution.py:104
  106.2 0.6 copy-done
  106.8 6.0 %fusion.28 = bf16[1,1,1,48,128,128]{5,3,4,2,1,0:T(8,128)(2,1)S(1)} fusion(f32[48]{0:T(128)S(1)} %copy-done.5, bf16[1,48,132,136]{3,1,2,0:T(8,128)(2,1)S(1)} %get-tuple-element.6, f32[128,128,48]{1,2,0:T(8,128)S(1)} %fusion.13, f32[128,128,48]{1,2,0:T(8,128)S(1)} %fusion.14, f32[128,128,48]{1,2,0:T(8,128)S(1)} %fusion.16, f32[128,128,48]{1,2,0:T(8,128)S(1)} %copy-done, ...), kind=kOutput, calls=%fused_computation.50 | convolution fusion | flops 83361792 | bytes 28324352 | tf_op jit(solution)/shard_map/hk,bkij->bhij/dot_general | solution.py:104
  112.7 1.6 %copy.17 = bf16[1,1,1,48,128,128]{5,4,3,2,1,0:T(8,128)(2,1)} copy(bf16[1,1,1,48,128,128]{5,3,4,2,1,0:T(8,128)(2,1)S(1)} %fusion.28) | data formatting | bytes 3145728 | tf_op jit(solution)/shard_map/broadcast_in_dim | solution.py:111
  (27 shorter events, 0.4 us)
Async XLA Ops:
  0.0 6.4 %collective-permute-start.1 = (bf16[1,1,64,128]{3,2,1,0:T(8,128)(2,1)}, bf16[1,1,64,128]{3,2,1,0:T(8,128)(2,1)S(1)}, u32[]{:S(2)}, u32[]{:S(2)}) collective-permute-start(bf16[1,1,64,128]{3,2,1,0:T(8,128)(2,1)} %param.5), channel_id=1, source_target_pairs={{2,0},{4,2},{6,4},{8,6},{10,8},{12,10},{14,12},{16,14},{18,16},{20... | collective-permute-start | bytes 49160 | tf_op jit(solution)/shard_map/ppermute | solution.py:10
  4.2 7.6 %collective-permute-start = (bf16[1,1,64,128]{3,2,1,0:T(8,128)(2,1)}, bf16[1,1,64,128]{3,2,1,0:T(8,128)(2,1)S(1)}, u32[]{:S(2)}, u32[]{:S(2)}) collective-permute-start(bf16[1,1,64,128]{3,2,1,0:T(8,128)(2,1)} %param.5), channel_id=1, source_target_pairs={{0,2},{2,4},{4,6},{6,8},{8,10},{10,12},{12,14},{14,16},{16,18},{18... | collective-permute-start | bytes 49160 | tf_op jit(solution)/shard_map/ppermute | solution.py:10
  7.1 5.8 %collective-permute-start.2 = (bf16[2,1,64,128]{3,2,1,0:T(8,128)(2,1)S(1)}, bf16[2,1,64,128]{3,2,1,0:T(8,128)(2,1)S(1)}, u32[]{:S(2)}, u32[]{:S(2)}) collective-permute-start(bf16[2,1,64,128]{3,2,1,0:T(8,128)(2,1)S(1)} %pad_maximum_fusion.4), channel_id=1, source_target_pairs={{4,0},{6,2},{8,4},{10,6},{12,8},{14,10},{16,12},{18,14},{20,16},{2... | collective-permute-start | bytes 98312 | tf_op jit(solution)/shard_map/ppermute | solution.py:10
  16.0 2.8 %copy-start.3 = (bf16[48,128,3,3]{1,0,3,2:T(8,128)(2,1)S(1)}, bf16[48,128,3,3]{1,0,3,2:T(8,128)(2,1)}, u32[]{:S(2)}) copy-start(bf16[48,128,3,3]{1,0,3,2:T(8,128)(2,1)} %param.6) | copy-start | bytes 331780
  37.9 3.3 %copy-start.4 = (f32[48]{0:T(128)S(1)}, f32[48]{0:T(128)}, u32[]{:S(2)}) copy-start(f32[48]{0:T(128)} %param.7) | copy-start | bytes 580
  51.6 19.0 %copy-start.2 = (bf16[48,48,3,3]{1,0,3,2:T(8,128)(2,1)S(1)}, bf16[48,48,3,3]{1,0,3,2:T(8,128)(2,1)}, u32[]{:S(2)}) copy-start(bf16[48,48,3,3]{1,0,3,2:T(8,128)(2,1)} %param.8) | copy-start | bytes 124420
  55.1 17.7 %collective-permute-start.5 = (bf16[1,48,128,4]{2,1,3,0:T(8,128)(2,1)S(1)}, bf16[1,48,128,4]{2,1,3,0:T(8,128)(2,1)S(1)}, u32[]{:S(2)}, u32[]{:S(2)}) collective-permute-start(bf16[1,48,128,4]{2,1,3,0:T(8,128)(2,1)S(1)} %copy.13), channel_id=1, source_target_pairs={{0,1},{1,2},{2,3},{3,4},{4,5},{5,6},{6,7},{7,8},{8,9},{9,10},{10,1... | collective-permute-start | bytes 147464 | tf_op jit(solution)/shard_map/ppermute | solution.py:10
  58.1 24.9 %collective-permute-start.6 = (bf16[1,48,128,4]{2,1,3,0:T(8,128)(2,1)S(1)}, bf16[1,48,128,4]{2,1,3,0:T(8,128)(2,1)S(1)}, u32[]{:S(2)}, u32[]{:S(2)}) collective-permute-start(bf16[1,48,128,4]{2,1,3,0:T(8,128)(2,1)S(1)} %copy.15), channel_id=1, source_target_pairs={{1,0},{2,1},{3,2},{4,3},{5,4},{6,5},{7,6},{8,7},{9,8},{10,9},{11,1... | collective-permute-start | bytes 147464 | tf_op jit(solution)/shard_map/ppermute | solution.py:10
  63.5 23.8 %collective-permute-start.7 = (bf16[1,48,4,128]{3,1,2,0:T(8,128)(2,1)}, bf16[1,48,4,128]{3,1,2,0:T(8,128)(2,1)}, u32[]{:S(2)}, u32[]{:S(2)}) collective-permute-start(bf16[1,48,4,128]{3,1,2,0:T(8,128)(2,1)} %get-tuple-element.10), channel_id=1, source_target_pairs={{1,0},{2,1},{3,2},{4,3},{5,4},{6,5},{7,6},{8,7},{9,8},{10,9},{11,1... | collective-permute-start | bytes 147464 | tf_op jit(solution)/shard_map/ppermute | solution.py:10
  66.7 20.7 %collective-permute-start.4 = (bf16[1,48,4,128]{3,1,2,0:T(8,128)(2,1)}, bf16[1,48,4,128]{3,1,2,0:T(8,128)(2,1)}, u32[]{:S(2)}, u32[]{:S(2)}) collective-permute-start(bf16[1,48,4,128]{3,1,2,0:T(8,128)(2,1)} %get-tuple-element.9), channel_id=1, source_target_pairs={{0,1},{1,2},{2,3},{3,4},{4,5},{5,6},{6,7},{7,8},{8,9},{9,10},{10,1... | collective-permute-start | bytes 147464 | tf_op jit(solution)/shard_map/ppermute | solution.py:10
  68.7 19.6 %collective-permute-start.3 = (bf16[1,48,4,4]{3,1,2,0:T(8,128)(2,1)}, bf16[1,48,4,4]{3,1,2,0:T(8,128)(2,1)S(1)}, u32[]{:S(2)}, u32[]{:S(2)}) collective-permute-start(bf16[1,48,4,4]{3,1,2,0:T(8,128)(2,1)} %get-tuple-element.7), channel_id=1, source_target_pairs={{0,2},{1,3},{2,4},{3,5},{4,6},{5,7},{6,8},{7,9},{8,10},{9,11},{10,... | collective-permute-start | bytes 4616 | tf_op jit(solution)/shard_map/ppermute | solution.py:10
  72.8 15.4 %collective-permute-start.8 = (bf16[1,48,4,4]{3,1,2,0:T(8,128)(2,1)}, bf16[1,48,4,4]{3,1,2,0:T(8,128)(2,1)S(1)}, u32[]{:S(2)}, u32[]{:S(2)}) collective-permute-start(bf16[1,48,4,4]{3,1,2,0:T(8,128)(2,1)} %get-tuple-element.8), channel_id=1, source_target_pairs={{2,0},{3,1},{4,2},{5,3},{6,4},{7,5},{8,6},{9,7},{10,8},{11,9},{12,... | collective-permute-start | bytes 4616 | tf_op jit(solution)/shard_map/ppermute | solution.py:10
  101.7 4.6 %copy-start.1 = (f32[128,128,48]{1,2,0:T(8,128)S(1)}, f32[128,128,48]{1,2,0:T(8,128)}, u32[]{:S(2)}) copy-start(f32[128,128,48]{1,2,0:T(8,128)} %fusion.20) | copy-start | bytes 9437188
  104.0 2.8 %copy-start = (f32[128,128,48]{1,2,0:T(8,128)S(1)}, f32[128,128,48]{1,2,0:T(8,128)}, u32[]{:S(2)}) copy-start(f32[128,128,48]{1,2,0:T(8,128)} %fusion.26) | copy-start | bytes 9437188
  104.0 2.8 %copy-start.5 = (f32[48]{0:T(128)S(1)}, f32[48]{0:T(128)}, u32[]{:S(2)}) copy-start(f32[48]{0:T(128)} %param.9) | copy-start | bytes 580
where the time goes:
time: 115 us; the launch traced here: 114 us
  matrix products  51.2 us (45%)
  starting transfers between devices  29.3 us (25%)
  other arithmetic  16.7 us (15%)
  local copies, waits for them, and re-layouts  14.1 us (12%)
  waiting for transfers between devices  2.7 us (2%)
    dot_general x9, matrix products, local(): jnp.einsum('hc,bcij->bhij', w_first[:, :, tap_row, tap_col], window_cells...  31.1 us
    ppermute x9, starting transfers between devices, from_behind(): return lax.ppermute(shard, axis, pairs)  29.3 us
    dot_general x9, matrix products, local(): jnp.einsum('hk,bkij->bhij', w_second[:, :, tap_row, tap_col], window_cell...  20.1 us
    concatenate x1, other arithmetic, local(): hidden = jnp.concatenate([upper, middle, lower], axis=2)  9.74 us
    slice x2, local copies, waits for them, and re-layouts, local(): left = neighbour(hidden[:, :, :, width - 4:], 1, offset > 0)  3.89 us
    ppermute x2, local copies, waits for them, and re-layouts, from_behind(): return lax.ppermute(shard, axis, pairs)  3.44 us
    select_n x1, other arithmetic, local(): jnp.where(outer_mask[None, None], features, jnp.zeros_like(features))  2.77 us
    ppermute x9, waiting for transfers between devices, from_behind(): return lax.ppermute(shard, axis, pairs)  2.7 us
  transfers between devices with their start and end apart: 9, of which 2 were waited for; matrix products, arithmetic and copies ran while one was open for 12% of the time, Pallas kernels for 0%

commit v1 on v0

v1 whole, which is shorter than its diff:
```python
import functools

import jax
import jax.numpy as jnp
from jax import lax
from jax.experimental import pallas as pl
from jax.experimental.pallas import tpu as pltpu
from jax.sharding import PartitionSpec as P

MESH = pl.DeviceIdType.MESH
TAPS = ((-1, -1, -1), (-1, -1, 0), (-1, 0, 0), (0, 0, 0), (0, 0, 1), (0, 1, 1), (1, 1, 1))
HOME = (-1, -1, 0, 0, 0, 1, 1)
FAR = -1e30
STEP = 4
ROWS = 16


def exchange(places, trunk_ref, side_ref, send_sem, recv_sem):
    row = lax.axis_index("diag")
    offset = lax.axis_index("off")
    shifts = [jnp.int32(-1), jnp.int32(1), offset - 1, offset, offset + 1]

    def inside(place):
        return (place >= 0) & (place < places)

    barrier = pltpu.get_barrier_semaphore()
    expected = jnp.int32(0)
    for slot, shift in enumerate(shifts):
        arrives = inside(row + shift) & (shift != 0)

        @pl.when(arrives)
        def _():
            pl.semaphore_signal(
                barrier, inc=1, device_id=(row + shift, offset), device_id_type=MESH
            )

        @pl.when(jnp.logical_not(inside(row + shift)))
        def _():
            side_ref[slot] = jnp.zeros_like(trunk_ref[...])

        @pl.when(shift == 0)
        def _():
            side_ref[slot] = trunk_ref[...]

        expected = expected + jnp.where(inside(row - shift) & (shift != 0), 1, 0)
    pl.semaphore_wait(barrier, expected)

    def copy(slot, target):
        return pltpu.make_async_remote_copy(
            src_ref=trunk_ref,
            dst_ref=side_ref.at[slot],
            send_sem=send_sem.at[slot],
            recv_sem=recv_sem.at[slot],
            device_id=(target, offset),
            device_id_type=MESH,
        )

    for slot, shift in enumerate(shifts):

        @pl.when(inside(row - shift) & (shift != 0))
        def _():
            copy(slot, row - shift).start()

    for slot, shift in enumerate(shifts):

        @pl.when(inside(row - shift) & (shift != 0))
        def _():
            copy(slot, row - shift).wait_send()

        @pl.when(inside(row + shift) & (shift != 0))
        def _():
            copy(slot, row + shift).wait_recv()


def pick(table, lanes):
    return jnp.take_along_axis(table, lanes, axis=1, mode="promise_in_bounds")


def column(row):
    size = row.shape[1]
    shape = (size, size)
    same = lax.broadcasted_iota(jnp.int32, shape, 0) == lax.broadcasted_iota(jnp.int32, shape, 1)
    return jnp.sum(jnp.where(same, row, 0.0), axis=1, keepdims=True)


def head(places, offsets, trunk_ref, side_ref, w1_ref, b1_ref, w2_ref, b2_ref, out_ref,
         rows_ref, cols_ref, one_ref, two_ref, acc_ref):
    channels, width = trunk_ref.shape
    hid = w1_ref.shape[2]
    row = lax.axis_index("diag")
    offset = lax.axis_index("off")
    line = 2 * width

    def in_band(up, across):
        gap = offset + across - up
        ok = (row + up >= 0) & (row + up < places)
        ok = ok & (row + offset + across >= 0) & (row + offset + across < places)
        return jnp.where(ok & (gap >= 0) & (gap < offsets), 1.0, 0.0).astype(jnp.float32)

    band = {(a, b): in_band(a, b) for a in (-1, 0, 1) for b in (-1, 0, 1)}
    at = lax.broadcasted_iota(jnp.int32, (1, line), 1)

    def by_place(shift, low, mid, high):
        return jnp.where(at < 4 - shift, low, jnp.where(at < 4 - shift + width, mid, high))

    def shifted(before, own, after):
        whole = jnp.concatenate([before, own, after], axis=1).astype(jnp.float32)
        return [
            whole[:, width - 6 + 2 * tap : width - 6 + 2 * tap + line].astype(jnp.bfloat16)
            for tap in range(3)
        ]

    blank = jnp.zeros((channels, line), jnp.bfloat16)
    row_x = shifted(side_ref[0], trunk_ref[...], side_ref[1])
    col_x = shifted(side_ref[2], side_ref[3], side_ref[4])
    row_terms, col_terms = {}, {}
    for tap in range(3):
        weights = jnp.concatenate([w1_ref[tap, v] for v in range(3)], axis=0)
        got = jnp.dot(weights, jnp.concatenate([row_x[tap], blank], axis=0),
                      preferred_element_type=jnp.float32)
        for v in range(3):
            row_terms[tap, v] = got[v * hid : (v + 1) * hid]
        weights = jnp.concatenate([w1_ref[u, tap] for u in range(3)], axis=0)
        got = jnp.dot(weights, jnp.concatenate([blank, col_x[tap]], axis=0),
                      preferred_element_type=jnp.float32)
        for u in range(3):
            col_terms[u, tap] = got[u * hid : (u + 1) * hid]

    row_sums, col_sums = {}, {}
    for side in (-1, 0, 1):
        row_keep = [by_place(2 * (t - 1), band[-1, side], band[0, side], band[1, side]) for t in range(3)]
        col_keep = [by_place(2 * (t - 1), band[side, -1], band[side, 0], band[side, 1]) for t in range(3)]
        for t in range(3):
            row_sums[t, side] = sum(row_keep[u] * row_terms[u, t] for u in range(3))
            col_sums[t, side] = sum(col_keep[v] * col_terms[t, v] for v in range(3))

    slot = lax.broadcasted_iota(jnp.int32, (hid, width), 1)
    blocks = rows_ref.shape[0]
    per = width // ROWS
    for block in range(blocks):
        start = (block // per) * width
        lanes = (block % per) * ROWS + slot % ROWS
        table = None
        for group in range(7):
            values = sum(row_sums[v, TAPS[group][v]][:, start : start + width] for v in range(3))
            values = pick(values, lanes)
            table = values if table is None else jnp.where(slot // ROWS == group, values, table)
        rows_ref[block] = table

    bias = column(b1_ref[...])
    for group in range(7):
        values = sum(col_sums[u, TAPS[group][u]] for u in range(3)) + bias
        kept = by_place(0, band[HOME[group], -1], band[HOME[group], 0], band[HOME[group], 1])
        values = jnp.where(kept > 0.5, values, FAR)
        for v in range(3):
            cols_ref[group, v * hid : (v + 1) * hid] = values[:, 4 * v : 4 * v + width]

    one_ref[...] = jnp.zeros_like(one_ref)
    two_ref[...] = jnp.zeros_like(two_ref)
    bias2 = column(b2_ref[...])

    def group_of(place):
        group = jnp.int32(0)
        for edge in (2, 4, 6, width + 2, width + 4, width + 6):
            group = group + jnp.where(place >= edge, 1, 0)
        return group

    picks = []
    for v in range(3):
        place = slot + 4 * v
        group = jnp.zeros_like(place)
        for edge in (2, 4, 6, width + 2, width + 4, width + 6):
            group = group + jnp.where(place >= edge, 1, 0)
        picks.append(group * ROWS)

    def chunk(base):
        columns = []
        for step in range(STEP):
            place = base + step
            table = rows_ref[place // ROWS]
            cols = cols_ref[group_of(place)]
            within = place % ROWS
            parts = [
                jnp.maximum(pick(table, picks[v] + within) + cols[v * hid : (v + 1) * hid], 0.0)
                for v in range(3)
            ]
            columns.append(jnp.concatenate(parts, axis=0).astype(jnp.bfloat16))
        got = jnp.dot(w2_ref[...], jnp.concatenate(columns, axis=1),
                      preferred_element_type=jnp.float32)
        done = two_ref[...] + got[2 * hid :] + bias2
        two_ref[...] = one_ref[...] + got[hid : 2 * hid]
        one_ref[...] = got[:hid]
        for step in range(STEP):
            acc_ref[pl.ds((base + step) * hid, hid)] = done[:, step * width : (step + 1) * width]

    chunk(jnp.int32(0))
    chunk(jnp.int32(STEP))

    @pl.loop(0, width // ROWS)
    def _(block):
        for step in range(ROWS // STEP):
            chunk(8 + block * ROWS + step * STEP)
        for h in range(hid):
            rows = acc_ref[pl.ds((8 + block * ROWS) * hid + h, ROWS, stride=hid), :]
            out_ref[h, pl.ds(pl.multiple_of(block * ROWS, ROWS), ROWS), :] = rows.astype(out_ref.dtype)


def local(places, offsets, trunk, w_first, b_first, w_second, b_second):
    channels, width = trunk.shape[2:]
    hid = w_first.shape[0]
    trunk = trunk.reshape(channels, width)
    vmem = pl.BlockSpec(memory_space=pltpu.VMEM)
    side = pl.pallas_call(
        functools.partial(exchange, places),
        out_shape=jax.ShapeDtypeStruct((5, channels, width), trunk.dtype),
        in_specs=[vmem],
        out_specs=vmem,
        scratch_shapes=[pltpu.SemaphoreType.DMA((5,)), pltpu.SemaphoreType.DMA((5,))],
        compiler_params=pltpu.CompilerParams(collective_id=0, has_side_effects=True),
        name="exchange",
    )(trunk)
    first = jnp.transpose(w_first, (2, 3, 0, 1))
    second = jnp.transpose(w_second, (2, 0, 3, 1)).reshape(3 * hid, 3 * hid)
    reach = width + 8
    result = pl.pallas_call(
        functools.partial(head, places, offsets),
        out_shape=jax.ShapeDtypeStruct((hid, width, width), jnp.bfloat16),
        in_specs=[vmem] * 6,
        out_specs=vmem,
        scratch_shapes=[
            pltpu.VMEM((pl.cdiv(reach, ROWS), hid, width), jnp.float32),
            pltpu.VMEM((7, 3 * hid, width), jnp.float32),
            pltpu.VMEM((hid, STEP * width), jnp.float32),
            pltpu.VMEM((hid, STEP * width), jnp.float32),
            pltpu.VMEM((reach * hid, width), jnp.float32),
        ],
        compiler_params=pltpu.CompilerParams(vmem_limit_bytes=32 * 1024 * 1024),
        name="head",
    )(trunk, side, first, b_first.reshape(1, hid), second, b_second.reshape(1, hid))
    return result[None, None, None]


def solution(mesh):
    placed = (P("diag", None, None, None), P(), P(), P(), P())
    return jax.shard_map(
        functools.partial(local, mesh.shape["diag"], mesh.shape["off"]),
        mesh=mesh,
        in_specs=placed,
        out_specs=P("diag", "off", None, None, None, None),
        check_vma=False,
    )
```

time: 115 us -> 23.9 us (0.21)
  the two profiles are of different devices: /device:TPU:24 before, /device:TPU:0 now
where the time goes in v1:
time: 23.9 us; the launch traced here: 23.5 us
  Pallas kernels  18.6 us (78%)
  local copies, waits for them, and re-layouts  4.88 us (20%)
    pallas_call x1, Pallas kernels, local(): pl.pallas_call(functools.partial(head, places, offsets), out_shape=jax.Sh...  10.5 us
    pallas_call x1, Pallas kernels, local(): pl.pallas_call(functools.partial(exchange, places), out_shape=jax.ShapeDt...  8.13 us
    unnamed x10, local copies, waits for them, and re-layouts  3.8 us
    transpose x1, local copies, waits for them, and re-layouts, local(): second = jnp.transpose(w_second, (2, 0, 3, 1)).reshape(3 * hid, 3 * hid)  0.96 us

profile of v1, /device:TPU:0, one launch (start us, length us, event | category | flops | bytes accessed | tf_op | source)
XLA Modules:
  0.0 23.5 jit_solution(282029516493155971)
XLA Ops:
  0.0 8.1 %exchange.1.side_ref = bf16[5,64,128]{2,1,0:T(8,128)(2,1)} custom-call(bf16[64,128]{1,0:T(8,128)(2,1)} %bitcast.7), custom_call_target="tpu_custom_call" | custom-call | tf_op jit(solution)/shard_map/exchange/pallas_call | solution.py:213
  8.1 1.0 %copy.7 = bf16[3,48,3,48]{3,2,1,0:T(4,128)(2,1)S(1)} copy(bf16[3,48,3,48]{3,1,2,0:T(8,128)(2,1)} %bitcast.11) | data formatting | bytes 82944 | tf_op jit(solution)/shard_map/transpose | solution.py:223
  9.1 0.1 reshape.14.w2_ref
  9.2 0.0 copy-start
  9.2 0.9 %copy-done = bf16[5,64,128]{2,1,0:T(8,128)(2,1)S(1)} copy-done((bf16[5,64,128]{2,1,0:T(8,128)(2,1)S(1)}, bf16[5,64,128]{2,1,0:T(8,128)(2,1)}, u32[]{:S(2)}) %copy-start) | copy-done | bytes 81944
  10.1 0.0 copy-start.1
  10.1 0.9 %copy-done.1 = bf16[48,128,3,3]{1,0,3,2:T(8,128)(2,1)S(1)} copy-done((bf16[48,128,3,3]{1,0,3,2:T(8,128)(2,1)S(1)}, bf16[48,128,3,3]{1,0,3,2:T(8,128)(2,1)}, u32[]{:S(2)}) %copy-start.1) | copy-done | bytes 110616
  11.0 0.0 copy-start.2
  11.0 0.7 %copy-done.2 = bf16[1,1,64,128]{3,2,1,0:T(8,128)(2,1)S(1)} copy-done((bf16[1,1,64,128]{3,2,1,0:T(8,128)(2,1)S(1)}, bf16[1,1,64,128]{3,2,1,0:T(8,128)(2,1)}, u32[]{:S(2)}) %copy-start.2) | copy-done | bytes 16408
  11.7 0.0 copy-start.3
  11.7 0.7 %copy-done.3 = f32[48]{0:T(128)S(1)} copy-done((f32[48]{0:T(128)S(1)}, f32[48]{0:T(128)}, u32[]{:S(2)}) %copy-start.3) | copy-done | bytes 216
  12.4 0.0 copy-start.4
  12.4 0.7 %copy-done.4 = f32[48]{0:T(128)S(1)} copy-done((f32[48]{0:T(128)S(1)}, f32[48]{0:T(128)}, u32[]{:S(2)}) %copy-start.4) | copy-done | bytes 216
  13.0 10.5 %head.1 = bf16[48,128,128]{2,1,0:T(8,128)(2,1)} custom-call(bf16[64,128]{1,0:T(8,128)(2,1)S(1)} %bitcast.8, bf16[5,64,128]{2,1,0:T(8,128)(2,1)S(1)} %copy-done, bf16[3,3,48,128]{3,2,1,0:T(8,128)(2,1)S(1)} %bitcast.6, f32[1,48]{1,0:T(1,128)S(1)} %bitcast.9, bf16[144,144]{1,0:T(8,128)(2,1)S(1)} %reshape.14.w2_ref, f32[1,48]{1,0:T(1,128)S(1)} %bitcast.10), custom_call_target="tpu_custom_call" | custom-call | tf_op jit(solution)/shard_map/head/pallas_call | solution.py:225
Async XLA Ops:
  9.2 0.9 %copy-start = (bf16[5,64,128]{2,1,0:T(8,128)(2,1)S(1)}, bf16[5,64,128]{2,1,0:T(8,128)(2,1)}, u32[]{:S(2)}) copy-start(bf16[5,64,128]{2,1,0:T(8,128)(2,1)} %exchange.1.side_ref) | copy-start | bytes 245764
  10.1 0.9 %copy-start.1 = (bf16[48,128,3,3]{1,0,3,2:T(8,128)(2,1)S(1)}, bf16[48,128,3,3]{1,0,3,2:T(8,128)(2,1)}, u32[]{:S(2)}) copy-start(bf16[48,128,3,3]{1,0,3,2:T(8,128)(2,1)} %param.6) | copy-start | bytes 331780
  11.0 0.7 %copy-start.2 = (bf16[1,1,64,128]{3,2,1,0:T(8,128)(2,1)S(1)}, bf16[1,1,64,128]{3,2,1,0:T(8,128)(2,1)}, u32[]{:S(2)}) copy-start(bf16[1,1,64,128]{3,2,1,0:T(8,128)(2,1)} %param.5) | copy-start | bytes 49156
  11.7 0.7 %copy-start.3 = (f32[48]{0:T(128)S(1)}, f32[48]{0:T(128)}, u32[]{:S(2)}) copy-start(f32[48]{0:T(128)} %param.7) | copy-start | bytes 580
  12.4 0.7 %copy-start.4 = (f32[48]{0:T(128)S(1)}, f32[48]{0:T(128)}, u32[]{:S(2)}) copy-start(f32[48]{0:T(128)} %param.9) | copy-start | bytes 580

commit v2 on v1

v2 whole, which is shorter than its diff:
```python
import functools

import jax
import jax.numpy as jnp
from jax import lax
from jax.experimental import pallas as pl
from jax.experimental.pallas import tpu as pltpu
from jax.sharding import PartitionSpec as P

MESH = pl.DeviceIdType.MESH
TAPS = ((-1, -1, -1), (-1, -1, 0), (-1, 0, 0), (0, 0, 0), (0, 0, 1), (0, 1, 1), (1, 1, 1))
HOME = (-1, -1, 0, 0, 0, 1, 1)
VARIANTS = ((0, 2, 3), (1, 3, 3), (2, 3, 3), (3, 3, 3), (3, 3, 4), (3, 3, 5), (3, 4, 6))
FAR = -1e30
SIDES = (-1, 0, 1)
EDGE = 8
STEP = 4
ROWS = 16


def exchange(places, own_ref, first_ref, second_ref, bias1_ref, bias2_ref,
             side_ref, w1_ref, w2_ref, b1_ref, b2_ref,
             trunk_ref, raw_ref, load_sem, send_sem, recv_sem):
    hid = raw_ref.shape[2]
    loads = [
        pltpu.make_async_copy(source, target, load_sem.at[i])
        for i, (source, target) in enumerate((
            (own_ref, trunk_ref), (second_ref, raw_ref), (first_ref, w1_ref),
            (bias1_ref, b1_ref), (bias2_ref, b2_ref),
        ))
    ]
    for load in loads:
        load.start()
    row = lax.axis_index("diag")
    offset = lax.axis_index("off")
    shifts = [jnp.int32(-1), jnp.int32(1), offset - 1, offset, offset + 1]

    def inside(place):
        return (place >= 0) & (place < places)

    barrier = pltpu.get_barrier_semaphore()
    for shift in shifts:
        arrives = inside(row + shift) & (shift != 0)

        @pl.when(arrives)
        def _():
            pl.semaphore_signal(
                barrier, inc=1, device_id=(row + shift, offset), device_id_type=MESH
            )

    loads[0].wait()
    expected = jnp.int32(0)
    for slot, shift in enumerate(shifts):

        @pl.when(jnp.logical_not(inside(row + shift)))
        def _():
            side_ref[slot] = jnp.zeros(trunk_ref.shape, trunk_ref.dtype)

        @pl.when(shift == 0)
        def _():
            side_ref[slot] = trunk_ref[...]

        expected = expected + jnp.where(inside(row - shift) & (shift != 0), 1, 0)
    pl.semaphore_wait(barrier, expected)

    def copy(slot, target):
        return pltpu.make_async_remote_copy(
            src_ref=trunk_ref,
            dst_ref=side_ref.at[slot],
            send_sem=send_sem.at[slot],
            recv_sem=recv_sem.at[slot],
            device_id=(target, offset),
            device_id_type=MESH,
        )

    for slot, shift in enumerate(shifts):

        @pl.when(inside(row - shift) & (shift != 0))
        def _():
            copy(slot, row - shift).start()

    side_ref[5] = trunk_ref[...]
    loads[1].wait()
    for u in range(3):
        taps = [raw_ref[u, v].astype(jnp.float32) for v in range(3)]
        w2_ref[u * hid : (u + 1) * hid] = jnp.concatenate(taps, axis=1).astype(w2_ref.dtype)
    for load in loads[2:]:
        load.wait()

    for slot, shift in enumerate(shifts):

        @pl.when(inside(row - shift) & (shift != 0))
        def _():
            copy(slot, row - shift).wait_send()

        @pl.when(inside(row + shift) & (shift != 0))
        def _():
            copy(slot, row + shift).wait_recv()


def column(row):
    size = row.shape[1]
    shape = (size, size)
    same = lax.broadcasted_iota(jnp.int32, shape, 0) == lax.broadcasted_iota(jnp.int32, shape, 1)
    return jnp.sum(jnp.where(same, row, 0.0), axis=1, keepdims=True)


def outer(left, right):
    return lax.dot_general(left, right, (((1,), (1,)), ((), ())), preferred_element_type=jnp.float32)


def head(places, offsets, side_ref, w1_ref, w2_ref, b1_ref, b2_ref, out_ref,
         rows_ref, cols_ref, one_ref, two_ref, acc_ref, tile_ref, out_sem):
    channels, width = side_ref.shape[1:]
    hid = w1_ref.shape[2]
    row = lax.axis_index("diag")
    offset = lax.axis_index("off")
    reach = width + 8

    def in_band(up, across):
        gap = offset + across - up
        ok = (row + up >= 0) & (row + up < places)
        ok = ok & (row + offset + across >= 0) & (row + offset + across < places)
        return jnp.where(ok & (gap >= 0) & (gap < offsets), 1.0, 0.0).astype(jnp.float32)

    band = {(a, b): in_band(a, b) for a in SIDES for b in SIDES}

    def by_place(at, shift, low, mid, high):
        return jnp.where(at < 4 - shift, low, jnp.where(at < 4 - shift + width, mid, high))

    whole = jnp.concatenate([
        jnp.concatenate([side_ref[0], side_ref[5], side_ref[1]], axis=1),
        jnp.concatenate([side_ref[2], side_ref[3], side_ref[4]], axis=1),
    ], axis=0).astype(jnp.float32).T
    bins = [whole[width - 6 + 2 * t : width - 6 + 2 * t + reach] for t in range(3)]
    lane = lax.broadcasted_iota(jnp.int32, (reach, 2 * channels), 1)
    at = lax.broadcasted_iota(jnp.int32, (reach, 2 * channels), 0)
    row_sums, col_sums = {}, {}
    row_left, col_left = [], []
    for side in SIDES:
        row_left.append(jnp.concatenate([
            bins[t] * jnp.where(lane < channels, by_place(
                at, 2 * (t - 1), band[-1, side], band[0, side], band[1, side]), 0.0)
            for t in range(3)], axis=1))
        col_left.append(jnp.concatenate([
            bins[t] * jnp.where(lane >= channels, by_place(
                at, 2 * (t - 1), band[side, -1], band[side, 0], band[side, 1]), 0.0)
            for t in range(3)], axis=1))
    row_left = jnp.concatenate(row_left, axis=0).astype(jnp.bfloat16)
    col_left = jnp.concatenate(col_left, axis=0).astype(jnp.bfloat16)
    for t in range(3):
        row_taps = jnp.concatenate([w1_ref[u, t] for u in range(3)], axis=1)
        col_taps = jnp.concatenate([w1_ref[t, v] for v in range(3)], axis=1)
        row_got = outer(row_left, jnp.concatenate([row_taps] * 3, axis=0))
        col_got = outer(col_left, jnp.concatenate([col_taps] * 3, axis=0))
        for i, side in enumerate(SIDES):
            row_sums[t, side] = row_got[i * reach : (i + 1) * reach]
            col_sums[t, side] = col_got[i * reach : (i + 1) * reach]

    wide = lax.broadcasted_iota(jnp.int32, (reach, 3 * hid), 1)

    def by_tap(first, mid, last):
        shape = first.shape
        return jnp.where(wide[: shape[0]] < hid, first, jnp.where(wide[: shape[0]] < 2 * hid, mid, last))

    row_terms = [sum(row_sums[v, TAPS[group][v]] for v in range(3)) for group in range(7)]
    for i, groups in enumerate(VARIANTS):
        rows_ref[i] = by_tap(*[row_terms[group] for group in groups])

    bias = jnp.concatenate([b1_ref[...]] * 3, axis=1)
    place = lax.broadcasted_iota(jnp.int32, (reach, 3 * hid), 0)
    for group in range(7):
        values = sum(col_sums[u, TAPS[group][u]] for u in range(3)) + bias
        kept = by_place(place, 0, band[HOME[group], -1], band[HOME[group], 0], band[HOME[group], 1])
        values = jnp.where(kept > 0.5, values, FAR)
        cols_ref[group] = by_tap(*[values[4 * v : 4 * v + width] for v in range(3)])

    one_ref[...] = jnp.zeros_like(one_ref)
    two_ref[...] = jnp.zeros_like(two_ref)
    bias2 = column(b2_ref[...])
    pair = lax.broadcasted_iota(jnp.int32, (EDGE, 3 * hid), 0) // 2

    def group_of(place):
        group = jnp.int32(0)
        for edge in (2, 4, 6, width + 2, width + 4, width + 6):
            group = group + jnp.where(place >= edge, 1, 0)
        return group

    def chunk(base):
        cells = []
        for step in range(STEP):
            place = base + step
            cols = cols_ref.at[group_of(place)]
            term = [rows_ref[i, pl.ds(place, 1), :] for i in range(7)]
            low = jnp.where(pair == 0, term[0], jnp.where(pair == 1, term[1], jnp.where(pair == 2, term[2], term[3])))
            high = jnp.where(pair == 3, term[6], jnp.where(pair == 2, term[5], jnp.where(pair == 1, term[4], term[3])))
            cells.append(cols[:EDGE] + low)
            cells.append(cols[EDGE : width - EDGE] + term[3])
            cells.append(cols[width - EDGE :] + high)
        hidden = jnp.maximum(jnp.concatenate(cells, axis=0), 0.0).astype(jnp.bfloat16)
        got = outer(w2_ref[...], hidden)
        done = two_ref[...] + got[2 * hid :] + bias2
        two_ref[...] = one_ref[...] + got[hid : 2 * hid]
        one_ref[...] = got[:hid]
        for step in range(STEP):
            acc_ref[pl.ds((base + step) * hid, hid)] = done[:, step * width : (step + 1) * width]

    chunk(jnp.int32(0))
    chunk(jnp.int32(STEP))

    def store(block):
        part = pl.ds(pl.multiple_of(block * ROWS, ROWS), ROWS)
        return pltpu.make_async_copy(tile_ref.at[:, part, :], out_ref.at[:, part, :], out_sem.at[block])

    @pl.loop(0, width // ROWS)
    def _(block):
        for step in range(ROWS // STEP):
            chunk(8 + block * ROWS + step * STEP)
        for h in range(hid):
            rows = acc_ref[pl.ds((8 + block * ROWS) * hid + h, ROWS, stride=hid), :]
            tile_ref[h, pl.ds(pl.multiple_of(block * ROWS, ROWS), ROWS), :] = rows.astype(tile_ref.dtype)
        store(block).start()

    for block in range(width // ROWS):
        store(block).wait()


def local(places, offsets, trunk, w_first, b_first, w_second, b_second):
    channels, width = trunk.shape[2:]
    hid = w_first.shape[0]
    trunk = trunk.reshape(channels, width)
    first = jnp.transpose(w_first, (2, 3, 0, 1))
    second = jnp.transpose(w_second, (2, 3, 0, 1))
    vmem = pl.BlockSpec(memory_space=pltpu.VMEM)
    hbm = pl.BlockSpec(memory_space=pltpu.HBM)
    limit = 40 * 1024 * 1024
    staged = pl.pallas_call(
        functools.partial(exchange, places),
        out_shape=(
            pltpu.VMEM((6, channels, width), trunk.dtype),
            pltpu.VMEM(first.shape, first.dtype),
            pltpu.VMEM((3 * hid, 3 * hid), second.dtype),
            pltpu.VMEM((1, hid), b_first.dtype),
            pltpu.VMEM((1, hid), b_second.dtype),
        ),
        in_specs=[hbm] * 5,
        out_specs=(vmem,) * 5,
        scratch_shapes=[
            pltpu.VMEM((channels, width), trunk.dtype),
            pltpu.VMEM(second.shape, second.dtype),
            pltpu.SemaphoreType.DMA((5,)),
            pltpu.SemaphoreType.DMA((5,)),
            pltpu.SemaphoreType.DMA((5,)),
        ],
        compiler_params=pltpu.CompilerParams(
            collective_id=0, has_side_effects=True, vmem_limit_bytes=limit
        ),
        name="exchange",
    )(*[pltpu.with_memory_space_constraint(a, pltpu.HBM) for a in (
        trunk, first, second, b_first.reshape(1, hid), b_second.reshape(1, hid))])
    reach = width + 8
    result = pl.pallas_call(
        functools.partial(head, places, offsets),
        out_shape=jax.ShapeDtypeStruct((hid, width, width), jnp.bfloat16),
        in_specs=[vmem] * 5,
        out_specs=hbm,
        scratch_shapes=[
            pltpu.VMEM((7, reach, 3 * hid), jnp.float32),
            pltpu.VMEM((7, width, 3 * hid), jnp.float32),
            pltpu.VMEM((hid, STEP * width), jnp.float32),
            pltpu.VMEM((hid, STEP * width), jnp.float32),
            pltpu.VMEM((reach * hid, width), jnp.float32),
            pltpu.VMEM((hid, width, width), jnp.bfloat16),
            pltpu.SemaphoreType.DMA((width // ROWS,)),
        ],
        compiler_params=pltpu.CompilerParams(vmem_limit_bytes=limit),
        name="head",
    )(*staged)
    return result[None, None, None]


def solution(mesh):
    placed = (P("diag", None, None, None), P(), P(), P(), P())
    return jax.shard_map(
        functools.partial(local, mesh.shape["diag"], mesh.shape["off"]),
        mesh=mesh,
        in_specs=placed,
        out_specs=P("diag", "off", None, None, None, None),
        check_vma=False,
    )
```

time: 23.9 us -> 14.2 us (0.59)
  local copies, waits for them, and re-layouts: 4.88 us -> 0 us
  Pallas kernels: 18.6 us -> 13.9 us
    unnamed x10 -> x0, local copies, waits for them, and re-layouts: 3.8 us -> none
    pallas_call x1, Pallas kernels: 10.5 us -> 7.09 us  [local(): pl.pallas_call(functools.partial(head, places, offsets), out_shape=jax.Sh...]
    pallas_call x1, Pallas kernels: 8.13 us -> 6.84 us  [local(): pl.pallas_call(functools.partial(exchange, places), out_shape=(pltpu.VMEM...]
    transpose x1 -> x0, local copies, waits for them, and re-layouts: 0.96 us -> none  [local(): second = jnp.transpose(w_second, (2, 0, 3, 1)).reshape(3 * hid, 3 * hid)]
where the time goes in v2:
time: 14.2 us; the launch traced here: 13.9 us
  Pallas kernels  13.9 us (98%)
    pallas_call x1, Pallas kernels, local(): pl.pallas_call(functools.partial(head, places, offsets), out_shape=jax.Sh...  7.09 us
    pallas_call x1, Pallas kernels, local(): pl.pallas_call(functools.partial(exchange, places), out_shape=(pltpu.VMEM...  6.84 us

profile of v2, /device:TPU:0, one launch (start us, length us, event | category | flops | bytes accessed | tf_op | source)
XLA Modules:
  0.0 13.9 jit_solution(15066497537886001141)
XLA Ops:
  0.0 6.8 %exchange.1 = (bf16[6,64,128]{2,1,0:T(8,128)(2,1)S(1)}, bf16[3,3,48,128]{3,2,1,0:T(8,128)(2,1)S(1)}, bf16[144,144]{1,0:T(8,128)(2,1)S(1)}, f32[1,48]{1,0:T(1,128)S(1)}, f32[1,48]{1,0:T(1,128)S(1)}) custom-call(bf16[64,128]{1,0:T(8,128)(2,1)} %bitcast.8, bf16[3,3,48,128]{3,2,1,0:T(8,128)(2,1)} %bitcast.6, bf16[3,3,48,48]{3,2,1,0:T(8,128)(2,1)} %bitcast.7, ...), custom_call_target="tpu_custom_call" | custom-call | tf_op jit(solution)/shard_map/exchange/pallas_call | solution.py:237
  6.8 7.1 %head.1 = bf16[48,128,128]{2,1,0:T(8,128)(2,1)} custom-call(bf16[6,64,128]{2,1,0:T(8,128)(2,1)S(1)} %get-tuple-element.10.side_ref, bf16[3,3,48,128]{3,2,1,0:T(8,128)(2,1)S(1)} %get-tuple-element.11.w1_ref, bf16[144,144]{1,0:T(8,128)(2,1)S(1)} %get-tuple-element.12.w2_ref, f32[1,48]{1,0:T(1,128)S(1)} %get-tuple-element.13.b1_ref, ...), custom_call_target="tpu_custom_call" | custom-call | tf_op jit(solution)/shard_map/head/pallas_call | solution.py:262

commit v3 on v2

--- a/solution.py
+++ b/solution.py
@@ -21,6 +21,23 @@
 def exchange(places, own_ref, first_ref, second_ref, bias1_ref, bias2_ref,
              side_ref, w1_ref, w2_ref, b1_ref, b2_ref,
              trunk_ref, raw_ref, load_sem, send_sem, recv_sem):
+    row = lax.axis_index("diag")
+    offset = lax.axis_index("off")
+    shifts = [jnp.int32(-1), jnp.int32(1), offset - 1, offset, offset + 1]
+
+    def inside(place):
+        return (place >= 0) & (place < places)
+
+    barrier = pltpu.get_barrier_semaphore()
+    for shift in shifts:
+        arrives = inside(row + shift) & (shift != 0)
+
+        @pl.when(arrives)
+        def _():
+            pl.semaphore_signal(
+                barrier, inc=1, device_id=(row + shift, offset), device_id_type=MESH
+            )
+
     hid = raw_ref.shape[2]
     loads = [
         pltpu.make_async_copy(source, target, load_sem.at[i])
@@ -31,35 +48,9 @@
     ]
     for load in loads:
         load.start()
-    row = lax.axis_index("diag")
-    offset = lax.axis_index("off")
-    shifts = [jnp.int32(-1), jnp.int32(1), offset - 1, offset, offset + 1]
-
-    def inside(place):
-        return (place >= 0) & (place < places)
-
-    barrier = pltpu.get_barrier_semaphore()
-    for shift in shifts:
-        arrives = inside(row + shift) & (shift != 0)
-
-        @pl.when(arrives)
-        def _():
-            pl.semaphore_signal(
-                barrier, inc=1, device_id=(row + shift, offset), device_id_type=MESH
-            )
-
     loads[0].wait()
     expected = jnp.int32(0)
-    for slot, shift in enumerate(shifts):
-
-        @pl.when(jnp.logical_not(inside(row + shift)))
-        def _():
-            side_ref[slot] = jnp.zeros(trunk_ref.shape, trunk_ref.dtype)
-
-        @pl.when(shift == 0)
-        def _():
-            side_ref[slot] = trunk_ref[...]
-
+    for shift in shifts:
         expected = expected + jnp.where(inside(row - shift) & (shift != 0), 1, 0)
     pl.semaphore_wait(barrier, expected)
 
@@ -80,6 +71,16 @@
             copy(slot, row - shift).start()
 
     side_ref[5] = trunk_ref[...]
+    for slot, shift in enumerate(shifts):
+
+        @pl.when(jnp.logical_not(inside(row + shift)))
+        def _():
+            side_ref[slot] = jnp.zeros(trunk_ref.shape, trunk_ref.dtype)
+
+        @pl.when(shift == 0)
+        def _():
+            side_ref[slot] = trunk_ref[...]
+
     loads[1].wait()
     for u in range(3):
         taps = [raw_ref[u, v].astype(jnp.float32) for v in range(3)]
@@ -133,24 +134,32 @@
         jnp.concatenate([side_ref[2], side_ref[3], side_ref[4]], axis=1),
     ], axis=0).astype(jnp.float32).T
     bins = [whole[width - 6 + 2 * t : width - 6 + 2 * t + reach] for t in range(3)]
-    lane = lax.broadcasted_iota(jnp.int32, (reach, 2 * channels), 1)
-    at = lax.broadcasted_iota(jnp.int32, (reach, 2 * channels), 0)
+    at = lax.broadcasted_iota(jnp.int32, (EDGE, 2 * channels), 0)
+
+    def scaled(values, shift, low, mid, high):
+        start = reach - EDGE
+        return jnp.concatenate([
+            values[:EDGE] * by_place(at, shift, low, mid, high),
+            values[EDGE:start] * mid,
+            values[start:] * by_place(at + start, shift, low, mid, high),
+        ], axis=0)
+
     row_sums, col_sums = {}, {}
     row_left, col_left = [], []
     for side in SIDES:
         row_left.append(jnp.concatenate([
-            bins[t] * jnp.where(lane < channels, by_place(
-                at, 2 * (t - 1), band[-1, side], band[0, side], band[1, side]), 0.0)
+            scaled(bins[t], 2 * (t - 1), band[-1, side], band[0, side], band[1, side])
             for t in range(3)], axis=1))
         col_left.append(jnp.concatenate([
-            bins[t] * jnp.where(lane >= channels, by_place(
-                at, 2 * (t - 1), band[side, -1], band[side, 0], band[side, 1]), 0.0)
+            scaled(bins[t], 2 * (t - 1), band[side, -1], band[side, 0], band[side, 1])
             for t in range(3)], axis=1))
     row_left = jnp.concatenate(row_left, axis=0).astype(jnp.bfloat16)
     col_left = jnp.concatenate(col_left, axis=0).astype(jnp.bfloat16)
+    lane = lax.broadcasted_iota(jnp.int32, (hid, 2 * channels), 1)
+    none = jnp.zeros((hid, 2 * channels), w1_ref.dtype)
     for t in range(3):
-        row_taps = jnp.concatenate([w1_ref[u, t] for u in range(3)], axis=1)
-        col_taps = jnp.concatenate([w1_ref[t, v] for v in range(3)], axis=1)
+        row_taps = jnp.concatenate([jnp.where(lane < channels, w1_ref[u, t], none) for u in range(3)], axis=1)
+        col_taps = jnp.concatenate([jnp.where(lane < channels, none, w1_ref[t, v]) for v in range(3)], axis=1)
         row_got = outer(row_left, jnp.concatenate([row_taps] * 3, axis=0))
         col_got = outer(col_left, jnp.concatenate([col_taps] * 3, axis=0))
         for i, side in enumerate(SIDES):
@@ -197,7 +206,7 @@
             cells.append(cols[:EDGE] + low)
             cells.append(cols[EDGE : width - EDGE] + term[3])
             cells.append(cols[width - EDGE :] + high)
-        hidden = jnp.maximum(jnp.concatenate(cells, axis=0), 0.0).astype(jnp.bfloat16)
+        hidden = jnp.maximum(jnp.concatenate(cells, axis=0).astype(jnp.bfloat16), jnp.bfloat16(0))
         got = outer(w2_ref[...], hidden)
         done = two_ref[...] + got[2 * hid :] + bias2
         two_ref[...] = one_ref[...] + got[hid : 2 * hid]
@@ -212,15 +221,26 @@
         part = pl.ds(pl.multiple_of(block * ROWS, ROWS), ROWS)
         return pltpu.make_async_copy(tile_ref.at[:, part, :], out_ref.at[:, part, :], out_sem.at[block])
 
-    @pl.loop(0, width // ROWS)
-    def _(block):
+    def chunks(block):
         for step in range(ROWS // STEP):
             chunk(8 + block * ROWS + step * STEP)
+
+    def release(block):
+        part = pl.ds(pl.multiple_of(block * ROWS, ROWS), ROWS)
         for h in range(hid):
             rows = acc_ref[pl.ds((8 + block * ROWS) * hid + h, ROWS, stride=hid), :]
-            tile_ref[h, pl.ds(pl.multiple_of(block * ROWS, ROWS), ROWS), :] = rows.astype(tile_ref.dtype)
+            tile_ref[h, part, :] = rows.astype(tile_ref.dtype)
         store(block).start()
 
+    blocks = width // ROWS
+    chunks(jnp.int32(0))
+
+    @pl.loop(1, blocks)
+    def _(block):
+        release(block - 1)
+        chunks(block)
+
+    release(jnp.int32(blocks - 1))
     for block in range(width // ROWS):
         store(block).wait()
 

time: 14.2 us -> 13.8 us (0.972)
  Pallas kernels: 13.9 us -> 13.6 us
    pallas_call x1, Pallas kernels: 7.09 us -> 6.73 us  [local(): pl.pallas_call(functools.partial(head, places, offsets), out_shape=jax.Sh...]
where the time goes in v3:
time: 13.8 us; the launch traced here: 13.6 us
  Pallas kernels  13.6 us (99%)
    pallas_call x1, Pallas kernels, local(): pl.pallas_call(functools.partial(exchange, places), out_shape=(pltpu.VMEM...  6.84 us
    pallas_call x1, Pallas kernels, local(): pl.pallas_call(functools.partial(head, places, offsets), out_shape=jax.Sh...  6.73 us

profile of v3, /device:TPU:0, one launch (start us, length us, event | category | flops | bytes accessed | tf_op | source)
XLA Modules:
  0.0 13.6 jit_solution(2607590422069521804)
XLA Ops:
  0.0 6.8 %exchange.1 = (bf16[6,64,128]{2,1,0:T(8,128)(2,1)S(1)}, bf16[3,3,48,128]{3,2,1,0:T(8,128)(2,1)S(1)}, bf16[144,144]{1,0:T(8,128)(2,1)S(1)}, f32[1,48]{1,0:T(1,128)S(1)}, f32[1,48]{1,0:T(1,128)S(1)}) custom-call(bf16[64,128]{1,0:T(8,128)(2,1)} %bitcast.8, bf16[3,3,48,128]{3,2,1,0:T(8,128)(2,1)} %bitcast.6, bf16[3,3,48,48]{3,2,1,0:T(8,128)(2,1)} %bitcast.7, ...), custom_call_target="tpu_custom_call" | custom-call | tf_op jit(solution)/shard_map/exchange/pallas_call | solution.py:257
  6.8 6.7 %head.1 = bf16[48,128,128]{2,1,0:T(8,128)(2,1)} custom-call(bf16[6,64,128]{2,1,0:T(8,128)(2,1)S(1)} %get-tuple-element.10.side_ref, bf16[3,3,48,128]{3,2,1,0:T(8,128)(2,1)S(1)} %get-tuple-element.11.w1_ref, bf16[144,144]{1,0:T(8,128)(2,1)S(1)} %get-tuple-element.12.w2_ref, f32[1,48]{1,0:T(1,128)S(1)} %get-tuple-element.13.b1_ref, ...), custom_call_target="tpu_custom_call" | custom-call | tf_op jit(solution)/shard_map/head/pallas_call | solution.py:282
